TPU v7x, 32 devices: a whole 2x2x4 slice. The times are simulated.
32 devices in a mesh: region: 4 (over x, core), unit: 8 (over z, y).
Axes of the slice: x: 2, y: 2, z: 4, core: 2. Of those that a mesh axis runs over, the one named last changes fastest.
Arguments:
- noisy: bfloat16 [8192, 2048], P(('region', 'unit')), may hold values from -6 to 6
- strategy: bfloat16 [2048, 2048], replicated, may hold values from -0.125 to 0.125
- county_hist: float32 [256, 2048], P(('region', 'unit')), may hold values from -24 to 24
- tract_county: int32 [8192], P(('region', 'unit')), may hold values from 0 to 255, as said below
- tract_owner: int32 [8192, 1], P(('region', 'unit')), may hold values from 0 to 31; in each aligned block of 256 rows (0 to 255, 256 to 511, ...) at most 16 rows name the same one
Outputs:
- released: bfloat16 [8192, 2048], P(('region', 'unit'))
- relaid: float32 [16384, 2048], P(('region', 'unit'))
Inputs may be any that keep to these rules, and one draw needn't show every extreme that they name: `tract_county`: every county has at least one tract; the tracts of region r (rows r * 256 * 8 onward) lie in counties of region r (rows r * 8 * 8 onward of county_hist). `tract_owner`: among the 256 rows of one device no owner appears more than 16 times, and some owner appears exactly 16 times.
All inputs are finite; a program needn't handle non-finite values.
Results may differ from a plain program's by a relative error of at most 0.005.
Values sent between devices are 32-bit elements; how exact they have to be, the bound alone decides.
A program may use at most 64 MiB of HBM per device.

v0:
```python
import functools

import jax
import jax.numpy as jnp
from jax import lax
from jax.experimental import pallas as pl
from jax.experimental.pallas import tpu as pltpu
from jax.sharding import PartitionSpec as P

STEP = 0.25
TILE = 256
LANES = 128
MESH = pl.DeviceIdType.MESH
f32, bf16, i32 = jnp.float32, jnp.bfloat16, jnp.int32


def dot_nn(a, b):
    return lax.dot_general(a, b, (((1,), (0,)), ((), ())), preferred_element_type=f32)


def dot_nt(a, b):
    return lax.dot_general(a, b, (((1,), (1,)), ((), ())), preferred_element_type=f32)


def halves(x):
    high = x.astype(bf16)
    return high, (x - high.astype(f32)).astype(bf16)


def kernel(
    regions,
    units,
    noisy_in,
    strategy,
    hist_in,
    county_in,
    owner_in,
    released,
    relaid,
    noisy,
    hist,
    county_row,
    owner_row,
    matrix,
    turned,
    field,
    rounded,
    misfit,
    partial,
    gathered,
    gaps,
    slots,
    mean_step,
    mean_misfit,
    input_sem,
    load_sem,
    sum_send,
    sum_recv,
    gap_send,
    gap_recv,
    row_send,
    row_recv,
    own_sem,
):
    devices = regions * units
    region, unit = lax.axis_index("region"), lax.axis_index("unit")
    me = region * units + unit
    rows, queries = noisy.shape
    width = strategy.shape[0]
    block = hist.shape[0]
    counties = units * block
    pitch = slots.shape[1]

    inputs = [
        pltpu.make_async_copy(source, target, input_sem.at[i])
        for i, (source, target) in enumerate(
            [(county_in, county_row), (noisy_in, noisy), (hist_in, hist), (owner_in, owner_row)]
        )
    ]
    for copy in inputs:
        copy.start()

    def load(i):
        part = pl.ds(pl.multiple_of(i * TILE, TILE), TILE)
        return pltpu.make_async_copy(strategy.at[part], matrix.at[part], load_sem.at[i])

    lax.fori_loop(0, width // TILE, lambda i, c: (load(i).start(), c)[1], 0)

    barrier = pltpu.get_barrier_semaphore()

    def greet(k, c):
        peer = lax.rem(me + k, devices)
        pl.semaphore_signal(
            barrier, inc=1, device_id=(peer // units, lax.rem(peer, units)), device_id_type=MESH
        )
        return c

    lax.fori_loop(1, devices, greet, 0)

    def columns(i):
        return pl.ds(pl.multiple_of(i * TILE, TILE), TILE)

    for copy in inputs:
        copy.wait()
    local_row = county_row[...] - region * counties
    member_row = (
        lax.broadcasted_iota(i32, (counties, rows), 0) == jnp.broadcast_to(local_row, (counties, rows))
    )
    member_sum = member_row.astype(f32).astype(bf16)


    def sums(i, c):
        partial[:, :, columns(i)] = dot_nn(member_sum, noisy[:, columns(i)]).reshape(
            units, block, TILE
        )
        return c

    lax.fori_loop(0, queries // TILE, sums, 0)
    tally = jnp.sum(member_row.astype(f32), axis=1, keepdims=True)
    partial[:, :, queries:] = jnp.broadcast_to(tally, (counties, LANES)).reshape(units, block, LANES)

    pl.semaphore_wait(barrier, devices - 1)

    def to_unit(k):
        return lax.rem(unit + k, units), lax.rem(unit + units - k, units)

    def sum_copy(k):
        peer, _ = to_unit(k)
        return pltpu.make_async_remote_copy(
            src_ref=partial.at[peer],
            dst_ref=gathered.at[k],
            send_sem=sum_send.at[k],
            recv_sem=sum_recv.at[k],
            device_id=(region, peer),
            device_id_type=MESH,
        )

    for k in range(1, units):
        sum_copy(k).start()

    def first(i, c):
        load(i).wait()
        flipped = matrix[columns(i), :].T
        turned[:, columns(i)] = flipped
        value = STEP * dot_nn(noisy[...], flipped)
        field[:, columns(i)] = value
        rounded[:, columns(i)] = value.astype(bf16)
        return c

    lax.fori_loop(0, width // TILE, first, 0)

    def second(i, c):
        misfit[:, columns(i)] = dot_nn(rounded[...], matrix[:, columns(i)]).astype(bf16)
        return c

    lax.fori_loop(0, queries // TILE, second, 0)

    def third(i, c):
        field[:, columns(i)] = 2.0 * field[:, columns(i)] - STEP * dot_nn(
            misfit[...], turned[:, columns(i)]
        )
        return c

    lax.fori_loop(0, width // TILE, third, 0)
    owners = owner_row[...]
    hits = lax.broadcasted_iota(i32, (devices, rows), 0) == jnp.broadcast_to(owners, (devices, rows))
    before = lax.broadcasted_iota(i32, (rows, rows), 0) < lax.broadcasted_iota(i32, (rows, rows), 1)
    earlier = dot_nn(hits.astype(f32).astype(bf16), before.astype(f32).astype(bf16))
    slot = jnp.sum(earlier * hits.astype(f32), axis=0, keepdims=True).astype(i32)
    target = owners * pitch + slot
    place = (
        lax.broadcasted_iota(i32, (devices * pitch, rows), 0)
        == jnp.broadcast_to(target, (devices * pitch, rows))
    ).astype(f32).astype(bf16)
    diagonal = (
        lax.broadcasted_iota(i32, (rows, rows), 0) == lax.broadcasted_iota(i32, (rows, rows), 1)
    ).astype(f32).astype(bf16)
    member_col = dot_nt(diagonal, member_sum).astype(bf16)
    place_twice = jnp.concatenate([place, place], axis=1)
    county_place = dot_nt(place, member_sum).astype(bf16)
    county_twice = jnp.concatenate([county_place, county_place], axis=1)
    member_twice = jnp.concatenate([member_col, member_col], axis=1)

    for k in range(1, units):
        sum_copy(k).wait()
    total = partial[unit]
    for k in range(1, units):
        total = total + gathered[k]
    count = total[:, queries : queries + 1]
    mean = (total[:, :queries] / count).astype(bf16)

    def wide(i):
        return pl.ds(pl.multiple_of(i * 2 * TILE, 2 * TILE), 2 * TILE)

    def mean_first(i, c):
        mean_step[:, wide(i)] = STEP * dot_nn(mean, turned[:, wide(i)])
        return c

    lax.fori_loop(0, width // (2 * TILE), mean_first, 0)

    def mean_second(i, c):
        mean_misfit[:, wide(i)] = dot_nn(mean_step[...].astype(bf16), matrix[:, wide(i)])
        return c

    lax.fori_loop(0, queries // (2 * TILE), mean_second, 0)

    def mean_third(i, c):
        moved = 2.0 * mean_step[:, wide(i)] - STEP * dot_nn(
            mean_misfit[...].astype(bf16), turned[:, wide(i)]
        )
        gaps[unit, :, wide(i)] = hist[:, wide(i)] / count - moved
        return c

    lax.fori_loop(0, width // (2 * TILE), mean_third, 0)

    def gap_copy(k, slot_at):
        peer, _ = to_unit(k)
        return pltpu.make_async_remote_copy(
            src_ref=gaps.at[slot_at],
            dst_ref=gaps.at[slot_at],
            send_sem=gap_send.at[k],
            recv_sem=gap_recv.at[k],
            device_id=(region, peer),
            device_id_type=MESH,
        )

    for k in range(1, units):
        gap_copy(k, unit).start()
    def spread(i, c):
        pair = jnp.concatenate(halves(field[:, columns(i)]), axis=0)
        slots[:, :, columns(i)] = dot_nn(place_twice, pair).reshape(devices, pitch, TILE)
        return c

    lax.fori_loop(0, width // TILE, spread, 0)

    for k in range(1, units):
        gap_copy(k, unit).wait_send()
        gap_copy(k, to_unit(k)[1]).wait_recv()

    def last(i, c):
        pair = jnp.concatenate(halves(gaps[:, :, columns(i)].reshape(counties, TILE)), axis=0)
        slots[:, :, columns(i)] += dot_nn(county_twice, pair).reshape(devices, pitch, TILE)
        return c

    lax.fori_loop(0, width // TILE, last, 0)

    def row_copy(k):
        peer = lax.rem(me + k, devices)
        return pltpu.make_async_remote_copy(
            src_ref=slots.at[peer],
            dst_ref=relaid.at[me],
            send_sem=row_send.at[k],
            recv_sem=row_recv.at[k],
            device_id=(peer // units, lax.rem(peer, units)),
            device_id_type=MESH,
        )

    lax.fori_loop(1, devices, lambda k, c: (row_copy(k).start(), c)[1], 0)
    own = pltpu.make_async_copy(slots.at[me], relaid.at[me], own_sem)
    own.start()

    def settle(i, c):
        pair = jnp.concatenate(halves(gaps[:, :, columns(i)].reshape(counties, TILE)), axis=0)
        rounded[:, columns(i)] = (field[:, columns(i)] + dot_nn(member_twice, pair)).astype(bf16)
        return c

    lax.fori_loop(0, width // TILE, settle, 0)

    def release(i, c):
        released[:, columns(i)] = dot_nn(rounded[...], matrix[:, columns(i)]).astype(bf16)
        return c

    lax.fori_loop(0, queries // TILE, release, 0)
    own.wait()

    def finish(k, c):
        row_copy(k).wait_send()
        source = lax.rem(me + devices - k, devices)
        pltpu.make_async_remote_copy(
            src_ref=slots.at[me],
            dst_ref=relaid.at[source],
            send_sem=row_send.at[k],
            recv_sem=row_recv.at[k],
            device_id=(source // units, lax.rem(source, units)),
            device_id_type=MESH,
        ).wait_recv()
        return c

    lax.fori_loop(1, devices, finish, 0)


def local(noisy, strategy, county_hist, tract_county, tract_owner):
    units, regions = lax.axis_size("unit"), lax.axis_size("region")
    devices = units * regions
    rows, queries = noisy.shape
    width = strategy.shape[0]
    block = county_hist.shape[0]
    capacity = 2 * rows // devices
    pitch = -(-capacity // 8) * 8
    vmem = pl.BlockSpec(memory_space=pltpu.VMEM)
    released, relaid = pl.pallas_call(
        functools.partial(kernel, regions, units),
        out_shape=(
            jax.ShapeDtypeStruct((rows, queries), bf16),
            jax.ShapeDtypeStruct((devices, pitch, width), f32),
        ),
        in_specs=[pl.BlockSpec(memory_space=pltpu.HBM)] * 5,
        out_specs=(vmem, vmem),
        scratch_shapes=[
            pltpu.VMEM((rows, queries), bf16),
            pltpu.VMEM((block, width), f32),
            pltpu.VMEM((1, rows), i32),
            pltpu.VMEM((1, rows), i32),
            pltpu.VMEM((width, queries), bf16),
            pltpu.VMEM((queries, width), bf16),
            pltpu.VMEM((rows, width), f32),
            pltpu.VMEM((rows, width), bf16),
            pltpu.VMEM((rows, queries), bf16),
            pltpu.VMEM((units, block, queries + LANES), f32),
            pltpu.VMEM((units, block, queries + LANES), f32),
            pltpu.VMEM((units, block, width), f32),
            pltpu.VMEM((devices, pitch, width), f32),
            pltpu.VMEM((block, width), f32),
            pltpu.VMEM((block, queries), f32),
            pltpu.SemaphoreType.DMA((4,)),
            pltpu.SemaphoreType.DMA((width // TILE,)),
            pltpu.SemaphoreType.DMA((units,)),
            pltpu.SemaphoreType.DMA((units,)),
            pltpu.SemaphoreType.DMA((units,)),
            pltpu.SemaphoreType.DMA((units,)),
            pltpu.SemaphoreType.DMA((devices,)),
            pltpu.SemaphoreType.DMA((devices,)),
            pltpu.SemaphoreType.DMA,
        ],
        compiler_params=pltpu.CompilerParams(
            collective_id=0, has_side_effects=True, vmem_limit_bytes=46 * 2**20
        ),
    )(
        noisy,
        strategy,
        county_hist,
        tract_county.reshape(1, rows),
        tract_owner.reshape(1, rows),
    )
    return released, relaid[:, :capacity].reshape(devices * capacity, width)


def solution(mesh):
    both = ("region", "unit")
    in_specs = (P(both, None), P(), P(both, None), P(both), P(both, None))
    return jax.shard_map(
        local, mesh=mesh, in_specs=in_specs, out_specs=(P(both, None), P(both, None)), check_vma=False
    )
```

profile of v0, /device:TPU:31, one launch (start us, length us, event | category | flops | bytes accessed | tf_op | source)
XLA Modules:
  0.0 137.9 jit_solution(11631091718893704201)
XLA Ops:
  0.6 0.0 copy-start
  0.6 1.2 copy-done
  1.9 0.0 copy-start.1
  1.9 0.8 copy-done.1
  2.7 0.0 copy-start.2
  2.7 0.7 copy-done.2
  3.4 0.0 copy-start.3
  3.4 0.7 copy-done.3
  4.1 130.8 %shard_map.68 = (bf16[256,2048]{1,0:T(8,128)(2,1)S(1)}, f32[32,16,2048]{2,1,0:T(8,128)S(1)}) custom-call(bf16[256,2048]{1,0:T(8,128)(2,1)S(1)} %copy-done, bf16[2048,2048]{1,0:T(8,128)(2,1)} %strategy.1, f32[8,2048]{1,0:T(8,128)S(1)} %copy-done.1, s32[1,256]{1,0:T(1,128)S(1)} %bitcast.4, s32[1,256]{1,0:T(1,128)S(1)} %bitcast.5), custom_call_target="tpu_custom_call" | custom-call | tf_op jit(solution)/shard_map/pallas_call | solution.py:301
  134.9 1.0 copy.9
  135.9 2.0 %copy.10 = f32[512,2048]{1,0:T(8,128)} copy(f32[512,2048]{1,0:T(8,128)S(1)} %bitcast.3) | data formatting | bytes 8388608
Async XLA Ops:
  0.6 1.2 copy-start
  1.9 0.8 copy-start.1
  2.7 0.7 copy-start.2
  3.4 0.7 copy-start.3
where the time goes:
time: 139 us; the launch traced here: 138 us
  Pallas kernels  131 us (94%)
  local copies, waits for them, and re-layouts  6.4 us (5%)
    pallas_call x1, Pallas kernels, local(): pl.pallas_call(functools.partial(kernel, regions, units), out_shape=(jax....  131 us
    unnamed x10, local copies, waits for them, and re-layouts  6.4 us

commit v1 on v0

--- a/solution.py
+++ b/solution.py
@@ -213,19 +213,27 @@
 
     lax.fori_loop(0, width // (2 * TILE), mean_third, 0)
 
-    def gap_copy(k, slot_at):
-        peer, _ = to_unit(k)
+    half = units // 2
+    base = unit // half * half
+    mirror = lax.rem(unit + half, units)
+
+    def gap_copy(which, slot_at, peer):
         return pltpu.make_async_remote_copy(
             src_ref=gaps.at[slot_at],
             dst_ref=gaps.at[slot_at],
-            send_sem=gap_send.at[k],
-            recv_sem=gap_recv.at[k],
+            send_sem=gap_send.at[which],
+            recv_sem=gap_recv.at[which],
             device_id=(region, peer),
             device_id_type=MESH,
         )
 
-    for k in range(1, units):
-        gap_copy(k, unit).start()
+    def ahead(k):
+        return base + lax.rem(unit - base + k, half)
+
+    gap_copy(0, unit, mirror).start()
+    for k in range(1, half):
+        gap_copy(k, unit, ahead(k)).start()
+
     def spread(i, c):
         pair = jnp.concatenate(halves(field[:, columns(i)]), axis=0)
         slots[:, :, columns(i)] = dot_nn(place_twice, pair).reshape(devices, pitch, TILE)
@@ -233,9 +241,16 @@
 
     lax.fori_loop(0, width // TILE, spread, 0)
 
-    for k in range(1, units):
-        gap_copy(k, unit).wait_send()
-        gap_copy(k, to_unit(k)[1]).wait_recv()
+    gap_copy(0, mirror, mirror).wait_recv()
+    for k in range(1, half):
+        gap_copy(half + k, mirror, ahead(k)).start()
+    gap_copy(0, unit, mirror).wait_send()
+    for k in range(1, half):
+        source = ahead(half - k)
+        gap_copy(k, unit, ahead(k)).wait_send()
+        gap_copy(k, source, source).wait_recv()
+        gap_copy(half + k, mirror, ahead(k)).wait_send()
+        gap_copy(half + k, lax.rem(source + half, units), source).wait_recv()
 
     def last(i, c):
         pair = jnp.concatenate(halves(gaps[:, :, columns(i)].reshape(counties, TILE)), axis=0)

time: 139 us -> 135 us (0.971)
  Pallas kernels: 131 us -> 128 us
    pallas_call x1, Pallas kernels: 131 us -> 128 us  [local(): pl.pallas_call(functools.partial(kernel, regions, units), out_shape=(jax....]
where the time goes in v1:
time: 135 us
  Pallas kernels  128 us (95%)
  local copies, waits for them, and re-layouts  6.4 us (5%)
    pallas_call x1, Pallas kernels, local(): pl.pallas_call(functools.partial(kernel, regions, units), out_shape=(jax....  128 us
    unnamed x10, local copies, waits for them, and re-layouts  6.4 us

profile of v1, /device:TPU:31, one launch (start us, length us, event | category | flops | bytes accessed | tf_op | source)
XLA Modules:
  0.0 134.6 jit_solution(6833768722224094644)
XLA Ops:
  0.6 0.0 copy-start
  0.6 1.2 copy-done
  1.9 0.0 copy-start.1
  1.9 0.8 copy-done.1
  2.7 0.0 copy-start.2
  2.7 0.7 copy-done.2
  3.4 0.0 copy-start.3
  3.4 0.7 copy-done.3
  4.1 127.5 %shard_map.68 = (bf16[256,2048]{1,0:T(8,128)(2,1)S(1)}, f32[32,16,2048]{2,1,0:T(8,128)S(1)}) custom-call(bf16[256,2048]{1,0:T(8,128)(2,1)S(1)} %copy-done, bf16[2048,2048]{1,0:T(8,128)(2,1)} %strategy.1, f32[8,2048]{1,0:T(8,128)S(1)} %copy-done.1, s32[1,256]{1,0:T(1,128)S(1)} %bitcast.4, s32[1,256]{1,0:T(1,128)S(1)} %bitcast.5), custom_call_target="tpu_custom_call" | custom-call | tf_op jit(solution)/shard_map/pallas_call | solution.py:316
  131.6 1.0 copy.9
  132.6 2.0 %copy.10 = f32[512,2048]{1,0:T(8,128)} copy(f32[512,2048]{1,0:T(8,128)S(1)} %bitcast.3) | data formatting | bytes 8388608
Async XLA Ops:
  0.6 1.2 copy-start
  1.9 0.8 copy-start.1
  2.7 0.7 copy-start.2
  3.4 0.7 copy-start.3

commit v2 on v1

--- a/solution.py
+++ b/solution.py
@@ -121,22 +121,30 @@
 
     pl.semaphore_wait(barrier, devices - 1)
 
-    def to_unit(k):
-        return lax.rem(unit + k, units), lax.rem(unit + units - k, units)
-
-    def sum_copy(k):
-        peer, _ = to_unit(k)
+    half = units // 2
+    base = unit // half * half
+    mirror = lax.rem(unit + half, units)
+
+    def ahead(k):
+        return base + lax.rem(unit - base + k, half)
+
+    def sum_copy(which, block_at, peer):
         return pltpu.make_async_remote_copy(
-            src_ref=partial.at[peer],
-            dst_ref=gathered.at[k],
-            send_sem=sum_send.at[k],
-            recv_sem=sum_recv.at[k],
+            src_ref=partial.at[block_at],
+            dst_ref=gathered.at[which],
+            send_sem=sum_send.at[which],
+            recv_sem=sum_recv.at[which],
             device_id=(region, peer),
             device_id_type=MESH,
         )
 
-    for k in range(1, units):
-        sum_copy(k).start()
+    def far_copy(k):
+        return sum_copy(half + k, lax.rem(ahead(k) + half, units), ahead(k))
+
+    for k in range(1, half):
+        far_copy(k).start()
+    for k in range(1, half):
+        sum_copy(k, ahead(k), ahead(k)).start()
 
     def first(i, c):
         load(i).wait()
@@ -154,6 +162,14 @@
         return c
 
     lax.fori_loop(0, queries // TILE, second, 0)
+
+    for k in range(1, half):
+        far_copy(k).wait()
+    beyond = partial[mirror]
+    for k in range(1, half):
+        beyond = beyond + gathered[half + k]
+    partial[mirror] = beyond
+    sum_copy(0, mirror, mirror).start()
 
     def third(i, c):
         field[:, columns(i)] = 2.0 * field[:, columns(i)] - STEP * dot_nn(
@@ -181,10 +197,11 @@
     county_twice = jnp.concatenate([county_place, county_place], axis=1)
     member_twice = jnp.concatenate([member_col, member_col], axis=1)
 
-    for k in range(1, units):
-        sum_copy(k).wait()
-    total = partial[unit]
-    for k in range(1, units):
+    sum_copy(0, mirror, mirror).wait()
+    for k in range(1, half):
+        sum_copy(k, ahead(k), ahead(k)).wait()
+    total = partial[unit] + gathered[0]
+    for k in range(1, half):
         total = total + gathered[k]
     count = total[:, queries : queries + 1]
     mean = (total[:, :queries] / count).astype(bf16)
@@ -212,10 +229,6 @@
         return c
 
     lax.fori_loop(0, width // (2 * TILE), mean_third, 0)
-
-    half = units // 2
-    base = unit // half * half
-    mirror = lax.rem(unit + half, units)
 
     def gap_copy(which, slot_at, peer):
         return pltpu.make_async_remote_copy(
@@ -226,9 +239,6 @@
             device_id=(region, peer),
             device_id_type=MESH,
         )
-
-    def ahead(k):
-        return base + lax.rem(unit - base + k, half)
 
     gap_copy(0, unit, mirror).start()
     for k in range(1, half):

time: 135 us -> 134 us (level)
  no operation moved by 1% of the time
where the time goes in v2:
time: 134 us
  Pallas kernels  127 us (95%)
  local copies, waits for them, and re-layouts  6.4 us (5%)
    pallas_call x1, Pallas kernels, local(): pl.pallas_call(functools.partial(kernel, regions, units), out_shape=(jax....  127 us
    unnamed x10, local copies, waits for them, and re-layouts  6.4 us

profile of v2, /device:TPU:31, one launch (start us, length us, event | category | flops | bytes accessed | tf_op | source)
XLA Modules:
  0.0 133.7 jit_solution(15823827644977106961)
XLA Ops:
  0.6 0.0 copy-start
  0.6 1.2 copy-done
  1.9 0.0 copy-start.1
  1.9 0.8 copy-done.1
  2.7 0.0 copy-start.2
  2.7 0.7 copy-done.2
  3.4 0.0 copy-start.3
  3.4 0.7 copy-done.3
  4.1 126.7 %shard_map.68 = (bf16[256,2048]{1,0:T(8,128)(2,1)S(1)}, f32[32,16,2048]{2,1,0:T(8,128)S(1)}) custom-call(bf16[256,2048]{1,0:T(8,128)(2,1)S(1)} %copy-done, bf16[2048,2048]{1,0:T(8,128)(2,1)} %strategy.1, f32[8,2048]{1,0:T(8,128)S(1)} %copy-done.1, s32[1,256]{1,0:T(1,128)S(1)} %bitcast.4, s32[1,256]{1,0:T(1,128)S(1)} %bitcast.5), custom_call_target="tpu_custom_call" | custom-call | tf_op jit(solution)/shard_map/pallas_call | solution.py:326
  130.7 1.0 copy.9
  131.7 2.0 %copy.10 = f32[512,2048]{1,0:T(8,128)} copy(f32[512,2048]{1,0:T(8,128)S(1)} %bitcast.3) | data formatting | bytes 8388608
Async XLA Ops:
  0.6 1.2 copy-start
  1.9 0.8 copy-start.1
  2.7 0.7 copy-start.2
  3.4 0.7 copy-start.3
